TPU v7x, 32 devices: a whole 2x2x4 slice. The times are simulated.
32 devices in a mesh: sp: 16 (over z, y, core), gz: 2 (over x).
Axes of the slice: x: 2, y: 2, z: 4, core: 2. Of those that a mesh axis runs over, the one named last changes fastest.
Arguments:
- volume: bfloat16 [128, 32, 8, 256], P(None, 'sp', 'gz'), may hold values from -6 to 6
- weight: bfloat16 [3, 3, 3, 64, 128], replicated, may hold values from -0.15625 to 0.15625
- cotangent: bfloat16 [128, 16, 4, 128], P(None, 'sp', 'gz'), may hold values from -6 to 6
Outputs:
- layer_out: bfloat16 [128, 16, 4, 128], P(None, 'sp', 'gz')
- volume_grad: bfloat16 [128, 32, 8, 256], P(None, 'sp', 'gz')
- kernel_grad: float32 [3, 3, 3, 64, 128], replicated
All inputs are finite; a program needn't handle non-finite values.
Results may differ from a plain program's by a relative error of at most 0.001.
Values may be sent and summed in bfloat16 or wider, within the bound.
No kernel may reach another device: no remote copies, remote signals or barrier semaphores. Data moves between devices by JAX's collectives and lax.ppermute only.
A program may use at most 64 MiB of HBM per device.

v0:
```python
import functools
import math

import jax
import jax.numpy as jnp
from jax import lax
from jax.experimental import pallas as pl
from jax.experimental.pallas import tpu as pltpu
from jax.sharding import PartitionSpec as P

GROUPS = 2
BF = jnp.bfloat16
F32 = jnp.float32
F16 = jnp.float16


def dot(left, right, dims=((1,), (0,))):
    return lax.dot_general(left, right, (dims, ((), ())), preferred_element_type=F32)


def exact(left, right):
    return dot(left, right).astype(BF)


def ones_where(shape, condition):
    row = lax.broadcasted_iota(jnp.int32, shape, 0)
    col = lax.broadcasted_iota(jnp.int32, shape, 1)
    return jnp.where(condition(row, col), 1.0, 0.0).astype(BF)


def rows_grouped(block, inner):
    size = block * inner
    return ones_where((size, size), lambda row, col: col == (row % block) * inner + row // block)


def rows_interleaved(block, inner):
    size = block * inner
    return ones_where((size, size), lambda row, col: row == (col % block) * inner + col // block)


def taps_of(parity):
    return (1,) if parity == 0 else (0, 2)


def cotangent_rows(source_ref, count):
    channels, _, out_y, out_x = source_ref.shape
    by_row = rows_grouped(channels, out_y)
    return exact(by_row[: count * channels], source_ref[...].reshape(channels * out_y, out_x))


def place():
    at_z, at_y = lax.axis_index("sp"), lax.axis_index("gz")
    return at_z % 2, at_z // 2 % 2 * lax.axis_size("gz") + at_y


def kept(array, flag):
    return jnp.where(flag != 0, array, jnp.zeros_like(array))


def put_rows(rows, cots_ref, first):
    _, channels, x_cells = cots_ref.shape
    out_x = x_cells // 2
    both = exact(
        rows,
        ones_where(
            (out_x, x_cells),
            lambda row, col: row == jnp.where(col < out_x, col, col - out_x + 1),
        ),
    )
    for k in range(rows.shape[0] // channels):
        cots_ref[first + k] = both[k * channels : (k + 1) * channels]


def lay_out_body(vol_ref, own_ref, class_ref, cots_ref):
    channels, z_cells, y_cells, x_cells = vol_ref.shape
    out_x = x_cells // 2
    lines = z_cells * y_cells
    block = 256 // lines
    put_rows(cotangent_rows(own_ref, cots_ref.shape[0]), cots_ref, 0)
    by_line = rows_grouped(block, lines)
    halves = ones_where(
        (x_cells, x_cells),
        lambda row, col: row == jnp.where(col < out_x, 2 * col, 2 * (col - out_x) + 1),
    )
    for at in range(0, channels, block):
        rows = vol_ref[at : at + block].reshape(block * lines, x_cells)
        rows = exact(exact(by_line, rows), halves)
        for z in range(z_cells):
            for y in range(y_cells):
                k = z * y_cells + y
                line = rows[k * block : (k + 1) * block]
                for x_par in range(2):
                    class_ref[
                        (z * 2 + y % 2) * 2 + x_par,
                        at : at + block,
                        y // 2 * out_x : (y // 2 + 1) * out_x,
                    ] = line[:, x_par * out_x : (x_par + 1) * out_x]


def kernel_grad_body(
    class_ref, own_ref, up_z_ref, up_y_ref, up_c_ref,
    cots_ref, keep_ref, send_ref, shift_ref, grad_ref,
):
    out_y, channels, _ = own_ref.shape
    width = channels // GROUPS

    cots_ref[:out_y] = own_ref[...]
    next_z = (lax.axis_index("sp") < lax.axis_size("sp") - 1) * 1
    next_y = (lax.axis_index("gz") < lax.axis_size("gz") - 1) * 1
    put_rows(kept(cotangent_rows(up_y_ref, 1), next_y), cots_ref, out_y)
    put_rows(kept(cotangent_rows(up_z_ref, out_y), next_z), cots_ref, out_y + 1)
    put_rows(kept(cotangent_rows(up_c_ref, 1), next_z * next_y), cots_ref, 2 * out_y + 1)
    pair_rows(cots_ref, shift_ref)

    first_half = lax.broadcasted_iota(jnp.int32, (width, channels), 1) < width
    for a in range(3):
        for b in range(3):
            for c in range(3):
                which = ((a != 1) * 2 + (b != 1)) * 2 + (c != 1)
                cot = ((a == 0) * 2 + (b == 0)) * 2 + (c == 0)
                full = dot(class_ref[which], shift_ref[cot], ((1,), (1,)))
                tap = (a * 3 + b) * 3 + c
                grad_ref[tap * width : (tap + 1) * width] = jnp.where(
                    first_half, full[:width], full[width:]
                )

    parts, padded, _ = keep_ref.shape
    half = grad_ref.shape[0] // 2
    each = half // parts
    top = jnp.maximum(jnp.max(jnp.abs(grad_ref[...])), 1e-30)
    level = jnp.floor(jnp.log2(jnp.full((padded - each, channels), top, F32))) - 14.0
    core, at = place()
    low = core == 0
    for part in range(parts):
        slot = at ^ part
        here = grad_ref[part * each : (part + 1) * each]
        there = grad_ref[half + part * each : half + (part + 1) * each]
        keep_ref[slot, :each] = jnp.where(low, here, there)
        send_ref[slot, :each] = jnp.where(low, there, here)
        keep_ref[slot, each:] = level
        send_ref[slot, each:] = level


def pair_rows(cots_ref, shift_ref):
    out_y = cots_ref.shape[0] // 2 - 1
    out_x = cots_ref.shape[2] // 2
    for plane in range(2):
        for off in range(2):
            for step in range(2):
                for y in range(out_y):
                    shift_ref[(plane * 2 + off) * 2 + step, :, y * out_x : (y + 1) * out_x] = cots_ref[
                        plane * (out_y + 1) + off + y, :, step * out_x : (step + 1) * out_x
                    ]


def spread_groups(weight_ref, spread_ref):
    _, width, channels = weight_ref.shape
    first_half = lax.broadcasted_iota(jnp.int32, (width, channels), 1) < width
    for tap in range(27):
        part = weight_ref[tap]
        zero = jnp.zeros_like(part)
        spread_ref[tap * channels : tap * channels + width] = jnp.where(first_half, part, zero)
        spread_ref[tap * channels + width : (tap + 1) * channels] = jnp.where(first_half, zero, part)


def forward_body(class_ref, from_z_ref, from_y_ref, weight_ref, out_ref, spread_ref, patch_ref):
    _, channels, cells = class_ref.shape
    out_x = from_y_ref.shape[2]
    out_y = cells // out_x
    spread_groups(weight_ref, spread_ref)
    moved = ones_where((out_x, out_x), lambda row, col: row == col - 1)

    def piece(a, q, x_par):
        if q < 0:
            return from_y_ref[a * 2 + x_par]
        lanes = slice(q // 2 * out_x, (q // 2 + 1) * out_x)
        if a == 0:
            return from_z_ref[q % 2 * 2 + x_par, :, lanes]
        return class_ref[((a - 1) * 2 + q % 2) * 2 + x_par, :, lanes]

    for a in range(3):
        for q in range(-1, 2 * out_y):
            odd = piece(a, q, 1)
            pieces = (exact(odd, moved), piece(a, q, 0), odd)
            for b in taps_of(q % 2):
                y = (q + 1 - b) // 2
                if 0 <= y < out_y:
                    for c in range(3):
                        tap = (a * 3 + b) * 3 + c
                        patch_ref[
                            tap * channels : (tap + 1) * channels, y * out_x : (y + 1) * out_x
                        ] = pieces[c]

    @pl.when(lax.axis_index("sp") == 0)
    def _():
        patch_ref[: 9 * channels] = jnp.zeros_like(patch_ref[: 9 * channels])

    @pl.when(lax.axis_index("gz") == 0)
    def _():
        for a in range(3):
            at = a * 9 * channels
            first = patch_ref.at[at : at + 3 * channels, :out_x]
            first[...] = jnp.zeros_like(first)

    result = dot(spread_ref[...], patch_ref[...], ((0,), (0,))).astype(BF)
    stacked = jnp.concatenate(
        [result[:, y * out_x : (y + 1) * out_x] for y in range(out_y)], axis=0
    )
    out_ref[...] = exact(rows_interleaved(channels, out_y), stacked).reshape(out_ref.shape)


def backward_body(cots_ref, weight_ref, grad_ref, spread_ref, shift_ref, lines_ref):
    channels, z_cells, y_cells, x_cells = grad_ref.shape
    lines = z_cells * y_cells
    out_x = x_cells // 2
    out_y = y_cells // 2
    spread_groups(weight_ref, spread_ref)
    pair_rows(cots_ref, shift_ref)

    for z in range(z_cells):
        for y_par in range(2):
            for x_par in range(2):
                total = jnp.zeros((channels, out_y * out_x), F32)
                for a in taps_of(z):
                    for b in taps_of(y_par):
                        for c in taps_of(x_par):
                            tap = (a * 3 + b) * 3 + c
                            cot = ((a == 0) * 2 + (b == 0)) * 2 + (c == 0)
                            total += dot(
                                spread_ref[tap * channels : (tap + 1) * channels], shift_ref[cot]
                            )
                total = total.astype(BF)
                for y in range(out_y):
                    lines_ref[
                        z * y_cells + 2 * y + y_par, :, x_par * out_x : (x_par + 1) * out_x
                    ] = total[:, y * out_x : (y + 1) * out_x]
    block = 256 // lines
    by_cell = rows_interleaved(block, lines)
    joined = ones_where(
        (x_cells, x_cells),
        lambda row, col: col == jnp.where(row < out_x, 2 * row, 2 * (row - out_x) + 1),
    )
    for at in range(0, channels, block):
        rows = jnp.concatenate([lines_ref[k, at : at + block, :] for k in range(lines)], axis=0)
        rows = exact(by_cell, exact(rows, joined))
        grad_ref[at : at + block] = rows.reshape(block, z_cells, y_cells, x_cells)


def assemble_body(scale, side, parts, each, *refs):
    slots, (out_ref, held_ref, half_ref, done) = refs[:parts], refs[-4:]
    core, mine = place()
    for k, slot_ref in enumerate(slots):
        held_ref[k] = slot_ref[:each] * (jnp.exp2(slot_ref[each : each + 1]) * scale)
    rows = parts * each
    start = (core ^ side) * rows
    split = parts if each % 8 == 0 else 1
    copies = []
    for at in range(0, rows, rows // split):
        for part in range(at // each, (at + rows // split) // each):
            half_ref[part * each : (part + 1) * each] = held_ref[mine ^ part]
        copies.append(
            pltpu.make_async_copy(
                half_ref.at[pl.ds(at, rows // split)],
                out_ref.at[pl.ds(pl.multiple_of(start + at, 8), rows // split)],
                done.at[len(copies)],
            )
        )
        copies[-1].start()
    for copy in copies:
        copy.wait()


def shifted(array, by_z, by_y):
    size_z, size_y = lax.axis_size("sp"), lax.axis_size("gz")
    pairs = [
        (z * size_y + y, (z + by_z) % size_z * size_y + (y + by_y) % size_y)
        for z in range(size_z)
        for y in range(size_y)
    ]
    return lax.ppermute(array, ("sp", "gz"), pairs)


def swapped(array, flip):
    return lax.ppermute(array, "sp", [(i, i ^ flip) for i in range(lax.axis_size("sp"))])


def swapped_in_plane(array, flip):
    size_z, size_y = lax.axis_size("sp"), lax.axis_size("gz")
    pairs = []
    for z in range(size_z):
        for y in range(size_y):
            to = ((z // 2 % 2) * size_y + y) ^ flip
            to_z = z // 4 * 4 + to // size_y * 2 + z % 2
            pairs.append((z * size_y + y, to_z * size_y + to % size_y))
    return lax.ppermute(array, ("sp", "gz"), pairs)


def coded(values, level, each):
    row = lax.broadcasted_iota(jnp.int32, values.shape, values.ndim - 2)
    return jnp.where(row < each, values * jnp.exp2(-level), level).astype(F16)


def decoded(message, each):
    message = message.astype(F32)
    level = message[..., each : each + 1, :]
    return message * jnp.exp2(level), level


def in_order(*arrays):
    return lax.optimization_barrier(arrays)


def partners(parts):
    return sorted(range(1, parts), key=lambda k: -bin(k).count("1"))


def sum_over_plane(keep, got, each, parts):
    level = jnp.maximum(keep[0, each : each + 1], got[0, each : each + 1]) + 1.0
    parts_got = {
        k: swapped_in_plane(coded(keep[k] + got[k], level, each), k) for k in partners(parts)
    }
    total = keep[0] + got[0]
    for k in partners(parts):
        values, its_level = decoded(parts_got[k], each)
        total = total + values
        level = jnp.maximum(level, its_level)
    return total, level + math.ceil(math.log2(parts))


def sum_over_lines(total, level, each):
    quads = lax.axis_size("sp") // 4
    message = coded(total, level, each)
    others = {k: swapped(message, 4 * k) for k in range(quads - 1, 0, -1)}
    terms = [decoded(message, each)] + [decoded(others[k], each) for k in range(1, quads)]
    while len(terms) > 1:
        terms = [
            (left[0] + right[0], jnp.maximum(left[1], right[1]) + 1.0)
            for left, right in zip(terms[::2], terms[1::2])
        ]
    return terms[0]


def spread_over_plane(total, level, each, parts):
    message = coded(total, level, each)
    slots = {k: swapped_in_plane(message, k) for k in partners(parts)}
    slots[0] = message
    return [slots[k] for k in range(parts)]


def call(body, outs, operands, scratch=(), flops=1_000_000, spaces=None):
    vmem = pl.BlockSpec(memory_space=pltpu.VMEM)
    return pl.pallas_call(
        body,
        out_shape=outs,
        in_specs=[
            pl.BlockSpec(memory_space=(spaces or {}).get(k, pltpu.VMEM))
            for k in range(len(operands))
        ],
        out_specs=jax.tree.map(lambda _: vmem, outs),
        scratch_shapes=scratch,
        compiler_params=pltpu.CompilerParams(vmem_limit_bytes=32 * 1024 * 1024),
        cost_estimate=pl.CostEstimate(flops=flops, bytes_accessed=4_000_000, transcendentals=0),
    )(*operands)


def per_device(volume, weight, cotangent):
    channels, z_cells, y_cells, x_cells = volume.shape
    slabs, pencils = lax.axis_size("sp"), lax.axis_size("gz")
    width = channels // GROUPS
    out_channels = weight.shape[4]
    out_z, out_y, out_x = cotangent.shape[1:]
    lines = z_cells * y_cells
    cells = out_y * out_x
    out_cells = slabs * pencils * out_z * out_y * out_x
    parts = 2 * pencils
    rows = 27 * width
    each = rows // 2 // parts
    padded = (each + 8) // 8 * 8
    shape = jax.ShapeDtypeStruct

    up_z = shifted(cotangent, -1, 0)
    up_c = shifted(cotangent, -1, -1)
    up_y = shifted(cotangent, 0, -1)
    classes, own = call(
        lay_out_body,
        (shape((8, channels, cells), BF), shape((out_y, channels, x_cells), BF)),
        (volume, cotangent),
        [],
        0,
    )
    share = shape((parts, padded, out_channels), F32)
    cots, keep, send = call(
        kernel_grad_body,
        (shape((2 * (out_y + 1), channels, x_cells), BF), share, share),
        (classes, own, up_z, up_y, up_c),
        [pltpu.VMEM((8, channels, cells), BF), pltpu.VMEM((rows, out_channels), F32)],
        500000000,
    )
    plane, send = in_order(classes[4:], send)
    from_z = shifted(plane, 1, 0)
    got = swapped(send, 1)
    weights = weight.reshape(27, width, out_channels)
    spread = pltpu.VMEM((27 * channels, out_channels), BF)
    volume_grad = call(
        backward_body,
        shape(volume.shape, BF),
        (cots, weights),
        [
            spread,
            pltpu.VMEM((8, channels, cells), BF),
            pltpu.VMEM((lines, channels, x_cells), BF),
        ],
        1_000_000_000,
    )
    total, level = sum_over_plane(keep, got, each, parts)
    total, volume_grad = in_order(total, volume_grad)
    total, from_z = in_order(total, from_z)
    edge = jnp.concatenate([from_z[2:], classes[2:4], classes[6:]], axis=0)[:, :, cells - out_x :]
    from_y = shifted(edge, 0, 1)
    total, level = sum_over_lines(total, level, each)
    mine = spread_over_plane(total, level, each, parts)
    output = call(
        forward_body,
        shape(cotangent.shape, BF),
        (classes, from_z, from_y, weights),
        [spread, pltpu.VMEM((27 * channels, cells), BF)],
        1_000_000_000,
    )
    mine, output = in_order(mine, output)
    other = swapped(jnp.stack(mine), 1)
    kernel_grad = None
    for side, half in enumerate((mine, other)):
        slots = [slot.astype(F32) for slot in half]
        kernel_grad = pl.pallas_call(
            functools.partial(assemble_body, 1.0 / math.sqrt(out_cells), side, parts, each),
            out_shape=shape((rows, out_channels), F32),
            in_specs=[pl.BlockSpec(memory_space=pltpu.VMEM)] * parts
            + [pl.BlockSpec(memory_space=pl.ANY)] * side,
            out_specs=pl.BlockSpec(memory_space=pl.ANY),
            scratch_shapes=[
                pltpu.VMEM((parts, each, out_channels), F32),
                pltpu.VMEM((rows // 2, out_channels), F32),
                pltpu.SemaphoreType.DMA((parts,)),
            ],
            input_output_aliases={parts: 0} if side else {},
            compiler_params=pltpu.CompilerParams(vmem_limit_bytes=32 * 1024 * 1024),
            cost_estimate=pl.CostEstimate(flops=1_000_000, bytes_accessed=1_000_000, transcendentals=0),
        )(*slots, *([kernel_grad] * side))
    kernel_grad = kernel_grad.reshape(weight.shape)
    return (output, volume_grad, kernel_grad)


def solution(mesh):
    in_specs = (P(None, "sp", "gz", None), P(), P(None, "sp", "gz", None))
    out_specs = (P(None, "sp", "gz", None), P(None, "sp", "gz", None), P())
    return jax.shard_map(
        per_device, mesh=mesh, in_specs=in_specs, out_specs=out_specs, check_vma=False
    )
```

profile of v0, /device:TPU:0, one launch (start us, length us, event | category | flops | bytes accessed | tf_op | source)
XLA Modules:
  0.0 40.3 jit_solution(13348146826734031826)
XLA Ops:
  0.6 5.5 %collective-permute-start = (bf16[128,1,2,128]{3,2,1,0:T(2,128)(2,1)}, bf16[128,1,2,128]{3,2,1,0:T(2,128)(2,1)S(1)}, u32[]{:S(2)}, u32[]{:S(2)}) collective-permute-start(bf16[128,1,2,128]{3,2,1,0:T(2,128)(2,1)} %own_ref.1), channel_id=1, source_target_pairs={{0,30},{1,31},{2,0},{3,1},{4,2},{5,3},{6,4},{7,5},{8,6},{9,7},{10,... | collective-permute-start | bytes 196616 | tf_op jit(solution)/shard_map/ppermute | solution.py:280
  6.1 1.5 %collective-permute-start.1 = (bf16[128,1,2,128]{3,2,1,0:T(2,128)(2,1)}, bf16[128,1,2,128]{3,2,1,0:T(2,128)(2,1)S(1)}, u32[]{:S(2)}, u32[]{:S(2)}) collective-permute-start(bf16[128,1,2,128]{3,2,1,0:T(2,128)(2,1)} %own_ref.1), channel_id=1, source_target_pairs={{0,1},{1,0},{2,3},{3,2},{4,5},{5,4},{6,7},{7,6},{8,9},{9,8},{10,11... | collective-permute-start | bytes 196616 | tf_op jit(solution)/shard_map/ppermute | solution.py:280
  8.0 1.0 %copy-done = bf16[128,2,4,256]{3,2,1,0:T(4,128)(2,1)S(1)} copy-done((bf16[128,2,4,256]{3,2,1,0:T(4,128)(2,1)S(1)}, bf16[128,2,4,256]{3,2,1,0:T(4,128)(2,1)}, u32[]{:S(2)}) %copy-start) | copy-done | bytes 524312
  9.0 0.8 %copy-done.1 = bf16[128,1,2,128]{3,2,1,0:T(2,128)(2,1)S(1)} copy-done((bf16[128,1,2,128]{3,2,1,0:T(2,128)(2,1)S(1)}, bf16[128,1,2,128]{3,2,1,0:T(2,128)(2,1)}, u32[]{:S(2)}) %copy-start.1) | copy-done | bytes 65560
  9.9 0.6 %shard_map.58 = (bf16[8,128,256]{2,1,0:T(8,128)(2,1)S(1)}, bf16[2,128,256]{2,1,0:T(8,128)(2,1)S(1)}) custom-call(bf16[128,2,4,256]{3,2,1,0:T(4,128)(2,1)S(1)} %copy-done, bf16[128,1,2,128]{3,2,1,0:T(2,128)(2,1)S(1)} %copy-done.1), custom_call_target="tpu_custom_call" | custom-call | bytes 4000000 | tf_op jit(solution)/shard_map/pallas_call | solution.py:352
  10.6 0.9 %collective-permute-done.2.up_c_ref = bf16[128,1,2,128]{3,2,1,0:T(2,128)(2,1)S(1)} collective-permute-done((bf16[128,1,2,128]{3,2,1,0:T(2,128)(2,1)}, bf16[128,1,2,128]{3,2,1,0:T(2,128)(2,1)S(1)}, u32[]{:S(2)}, u32[]{:S(2)}) %collective-permute-start.2) | collective-permute-done | bytes 65568 | tf_op jit(solution)/shard_map/ppermute | solution.py:280
  11.5 1.3 %shard_map.59 = (bf16[6,128,256]{2,1,0:T(8,128)(2,1)S(1)}, f32[4,224,128]{2,1,0:T(8,128)S(1)}, f32[4,224,128]{2,1,0:T(8,128)S(1)}) custom-call(bf16[8,128,256]{2,1,0:T(8,128)(2,1)S(1)} %get-tuple-element.19.class_ref, bf16[2,128,256]{2,1,0:T(8,128)(2,1)S(1)} %get-tuple-element.20.own_ref, bf16[128,1,2,128]{3,2,1,0:T(2,128)(2,1)S(1)} %collective-permute-done.up_z_ref, ...), custom_call_target="tpu_custom_call" | custom-call | flops 500000000 | bytes 4000000 | tf_op jit(solution)/shard_map/pallas_call | solution.py:352
  12.9 0.5 %collective-permute-start.7 = (bf16[4,128,256]{2,1,0:T(8,128)(2,1)S(1)}, bf16[4,128,256]{2,1,0:T(8,128)(2,1)S(1)}, u32[]{:S(2)}, u32[]{:S(2)}) collective-permute-start(bf16[4,128,256]{2,1,0:T(8,128)(2,1)S(1)} %slice.67), channel_id=1, source_target_pairs={{0,2},{1,3},{2,4},{3,5},{4,6},{5,7},{6,8},{7,9},{8,10},{9,11},{10,... | collective-permute-start | bytes 786440 | tf_op jit(solution)/shard_map/ppermute | solution.py:280
  13.5 1.2 %collective-permute-done.3 = f32[4,224,128]{2,1,0:T(8,128)S(1)} collective-permute-done((f32[4,224,128]{2,1,0:T(8,128)S(1)}, f32[4,224,128]{2,1,0:T(8,128)S(1)}, u32[]{:S(2)}, u32[]{:S(2)}) %collective-permute-start.3) | collective-permute-done | bytes 458784 | tf_op jit(solution)/shard_map/ppermute | solution.py:284
  14.9 1.3 %collective-permute-start.5 = (f16[224,128]{1,0:T(8,128)(2,1)S(1)}, f16[224,128]{1,0:T(8,128)(2,1)S(1)}, u32[]{:S(2)}, u32[]{:S(2)}) collective-permute-start(f16[224,128]{1,0:T(8,128)(2,1)S(1)} %get-tuple-element.45), channel_id=1, source_target_pairs={{0,1},{1,0},{2,3},{3,2},{4,5},{5,4},{6,7},{7,6},{8,9},{9,8},{10,11... | collective-permute-start | bytes 172040 | tf_op jit(solution)/shard_map/ppermute | solution.py:295
  16.2 2.2 %collective-permute-start.4 = (f16[224,128]{1,0:T(8,128)(2,1)S(1)}, f16[224,128]{1,0:T(8,128)(2,1)S(1)}, u32[]{:S(2)}, u32[]{:S(2)}) collective-permute-start(f16[224,128]{1,0:T(8,128)(2,1)S(1)} %get-tuple-element.43), channel_id=1, source_target_pairs={{0,5},{1,4},{2,7},{3,6},{4,1},{5,0},{6,3},{7,2},{8,13},{9,12},{10,... | collective-permute-start | bytes 172040 | tf_op jit(solution)/shard_map/ppermute | solution.py:295
  18.4 2.3 %shard_map.60 = bf16[128,2,4,256]{3,2,1,0:T(4,128)(2,1)} custom-call(bf16[6,128,256]{2,1,0:T(8,128)(2,1)S(1)} %get-tuple-element.24.cots_ref, bf16[27,64,128]{2,1,0:T(8,128)(2,1)S(1)} %bitcast.89), custom_call_target="tpu_custom_call" | custom-call | flops 1000000000 | bytes 4000000 | tf_op jit(solution)/shard_map/pallas_call | solution.py:352
  20.6 2.5 %collective-permute-done.6 = f16[224,128]{1,0:T(8,128)(2,1)S(1)} collective-permute-done((f16[224,128]{1,0:T(8,128)(2,1)S(1)}, f16[224,128]{1,0:T(8,128)(2,1)S(1)}, u32[]{:S(2)}, u32[]{:S(2)}) %collective-permute-start.6) | collective-permute-done | bytes 57376 | tf_op jit(solution)/shard_map/ppermute | solution.py:295
  23.3 2.0 %collective-permute-start.10 = (f16[224,128]{1,0:T(8,128)(2,1)S(1)}, f16[224,128]{1,0:T(8,128)(2,1)S(1)}, u32[]{:S(2)}, u32[]{:S(2)}) collective-permute-start(f16[224,128]{1,0:T(8,128)(2,1)S(1)} %get-tuple-element.38), channel_id=1, source_target_pairs={{0,24},{2,26},{4,28},{6,30},{8,16},{10,18},{12,20},{14,22},{16,8},... | collective-permute-start | bytes 172040 | tf_op jit(solution)/shard_map/ppermute | solution.py:284
  25.4 2.4 %collective-permute-start.8 = (f16[224,128]{1,0:T(8,128)(2,1)S(1)}, f16[224,128]{1,0:T(8,128)(2,1)S(1)}, u32[]{:S(2)}, u32[]{:S(2)}) collective-permute-start(f16[224,128]{1,0:T(8,128)(2,1)S(1)} %get-tuple-element.38), channel_id=1, source_target_pairs={{0,8},{2,10},{4,12},{6,14},{8,0},{10,2},{12,4},{14,6},{16,24},{18,... | collective-permute-start | bytes 172040 | tf_op jit(solution)/shard_map/ppermute | solution.py:284
  27.9 1.3 %collective-permute-start.14 = (bf16[6,128,128]{2,1,0:T(8,128)(2,1)S(1)}, bf16[6,128,128]{2,1,0:T(8,128)(2,1)S(1)}, u32[]{:S(2)}, u32[]{:S(2)}) collective-permute-start(bf16[6,128,128]{2,1,0:T(8,128)(2,1)S(1)} %pad_maximum_fusion.1), channel_id=1, source_target_pairs={{0,1},{1,0},{2,3},{3,2},{4,5},{5,4},{6,7},{7,6},{8,9},{9,8},{10,11... | collective-permute-start | bytes 589832 | tf_op jit(solution)/shard_map/ppermute | solution.py:280
  29.7 1.2 %collective-permute-done.9 = f16[224,128]{1,0:T(8,128)(2,1)S(1)} collective-permute-done((f16[224,128]{1,0:T(8,128)(2,1)S(1)}, f16[224,128]{1,0:T(8,128)(2,1)S(1)}, u32[]{:S(2)}, u32[]{:S(2)}) %collective-permute-start.9) | collective-permute-done | bytes 57376 | tf_op jit(solution)/shard_map/ppermute | solution.py:284
  31.0 1.6 %collective-permute-start.11 = (f16[224,128]{1,0:T(8,128)(2,1)S(1)}, f16[224,128]{1,0:T(8,128)(2,1)S(1)}, u32[]{:S(2)}, u32[]{:S(2)}) collective-permute-start(f16[224,128]{1,0:T(8,128)(2,1)S(1)} %select_convert_fusion), channel_id=1, source_target_pairs={{0,1},{1,0},{2,3},{3,2},{4,5},{5,4},{6,7},{7,6},{8,9},{9,8},{10,11... | collective-permute-start | bytes 172040 | tf_op jit(solution)/shard_map/ppermute | solution.py:295
  32.7 1.9 %collective-permute-start.13 = (f16[224,128]{1,0:T(8,128)(2,1)S(1)}, f16[224,128]{1,0:T(8,128)(2,1)S(1)}, u32[]{:S(2)}, u32[]{:S(2)}) collective-permute-start(f16[224,128]{1,0:T(8,128)(2,1)S(1)} %select_convert_fusion), channel_id=1, source_target_pairs={{0,5},{1,4},{2,7},{3,6},{4,1},{5,0},{6,3},{7,2},{8,13},{9,12},{10,... | collective-permute-start | bytes 172040 | tf_op jit(solution)/shard_map/ppermute | solution.py:295
  34.6 1.9 %shard_map.61 = bf16[128,1,2,128]{3,2,1,0:T(2,128)(2,1)} custom-call(bf16[8,128,256]{2,1,0:T(8,128)(2,1)S(1)} %get-tuple-element.19.class_ref, bf16[4,128,256]{2,1,0:T(8,128)(2,1)S(1)} %collective-permute-done.7.from_z_ref, bf16[6,128,128]{2,1,0:T(8,128)(2,1)S(1)} %collective-permute-done.14.from_y_ref, bf16[27,64,128]{2,1,0:T(8,128)(2,1)S(1)} %bitcast.90), custom_call_target="tpu_custom_call" | custom-call | flops 1000000000 | bytes 4000000 | tf_op jit(solution)/shard_map/pallas_call | solution.py:352
  36.8 1.0 %collective-permute-done.13 = f16[224,128]{1,0:T(8,128)(2,1)S(1)} collective-permute-done((f16[224,128]{1,0:T(8,128)(2,1)S(1)}, f16[224,128]{1,0:T(8,128)(2,1)S(1)}, u32[]{:S(2)}, u32[]{:S(2)}) %collective-permute-start.13) | collective-permute-done | bytes 57376 | tf_op jit(solution)/shard_map/ppermute | solution.py:295
  38.0 0.8 %shard_map.62.refs_4_ = f32[1728,128]{1,0:T(8,128)} custom-call(f32[224,128]{1,0:T(8,128)S(1)} %convert_element_type.88.refs_0_, f32[224,128]{1,0:T(8,128)S(1)} %convert_element_type.89.refs_1_, f32[224,128]{1,0:T(8,128)S(1)} %convert_element_type.90.refs_2_, f32[224,128]{1,0:T(8,128)S(1)} %convert_element_type.91.refs_3_), custom_call_target="tpu_custom_call" | custom-call | flops 1000000 | bytes 1000000 | tf_op jit(solution)/shard_map/pallas_call | solution.py:434
  38.9 0.6 %collective-permute-done.15 = f16[4,224,128]{2,1,0:T(8,128)(2,1)S(1)} collective-permute-done((f16[4,224,128]{2,1,0:T(8,128)(2,1)S(1)}, f16[4,224,128]{2,1,0:T(8,128)(2,1)S(1)}, u32[]{:S(2)}, u32[]{:S(2)}) %collective-permute-start.15) | collective-permute-done | bytes 229408 | tf_op jit(solution)/shard_map/ppermute | solution.py:284
  39.5 0.8 %shard_map.63 = f32[1728,128]{1,0:T(8,128)} custom-call(f32[224,128]{1,0:T(8,128)S(1)} %get-tuple-element.51.refs_0_, f32[224,128]{1,0:T(8,128)S(1)} %get-tuple-element.50.refs_1_, f32[224,128]{1,0:T(8,128)S(1)} %get-tuple-element.49.refs_2_, f32[224,128]{1,0:T(8,128)S(1)} %get-tuple-element.48.refs_3_, ...), custom_call_target="tpu_custom_call", output_to_operand_aliasing={{}: (4, {})} | custom-call | flops 1000000 | bytes 1000000 | tf_op jit(solution)/shard_map/pallas_call | solution.py:434
  (44 shorter events, 2.3 us)
Async XLA Ops:
  0.6 9.9 %collective-permute-start = (bf16[128,1,2,128]{3,2,1,0:T(2,128)(2,1)}, bf16[128,1,2,128]{3,2,1,0:T(2,128)(2,1)S(1)}, u32[]{:S(2)}, u32[]{:S(2)}) collective-permute-start(bf16[128,1,2,128]{3,2,1,0:T(2,128)(2,1)} %own_ref.1), channel_id=1, source_target_pairs={{0,30},{1,31},{2,0},{3,1},{4,2},{5,3},{6,4},{7,5},{8,6},{9,7},{10,... | collective-permute-start | bytes 196616 | tf_op jit(solution)/shard_map/ppermute | solution.py:280
  6.1 4.5 %collective-permute-start.1 = (bf16[128,1,2,128]{3,2,1,0:T(2,128)(2,1)}, bf16[128,1,2,128]{3,2,1,0:T(2,128)(2,1)S(1)}, u32[]{:S(2)}, u32[]{:S(2)}) collective-permute-start(bf16[128,1,2,128]{3,2,1,0:T(2,128)(2,1)} %own_ref.1), channel_id=1, source_target_pairs={{0,1},{1,0},{2,3},{3,2},{4,5},{5,4},{6,7},{7,6},{8,9},{9,8},{10,11... | collective-permute-start | bytes 196616 | tf_op jit(solution)/shard_map/ppermute | solution.py:280
  7.6 3.9 %collective-permute-start.2 = (bf16[128,1,2,128]{3,2,1,0:T(2,128)(2,1)}, bf16[128,1,2,128]{3,2,1,0:T(2,128)(2,1)S(1)}, u32[]{:S(2)}, u32[]{:S(2)}) collective-permute-start(bf16[128,1,2,128]{3,2,1,0:T(2,128)(2,1)} %own_ref.1), channel_id=1, source_target_pairs={{0,31},{1,30},{2,1},{3,0},{4,3},{5,2},{6,5},{7,4},{8,7},{9,6},{10,... | collective-permute-start | bytes 196616 | tf_op jit(solution)/shard_map/ppermute | solution.py:280
  8.0 1.0 %copy-start = (bf16[128,2,4,256]{3,2,1,0:T(4,128)(2,1)S(1)}, bf16[128,2,4,256]{3,2,1,0:T(4,128)(2,1)}, u32[]{:S(2)}) copy-start(bf16[128,2,4,256]{3,2,1,0:T(4,128)(2,1)} %vol_ref.1) | copy-start | bytes 1572868
  9.0 0.8 %copy-start.1 = (bf16[128,1,2,128]{3,2,1,0:T(2,128)(2,1)S(1)}, bf16[128,1,2,128]{3,2,1,0:T(2,128)(2,1)}, u32[]{:S(2)}) copy-start(bf16[128,1,2,128]{3,2,1,0:T(2,128)(2,1)} %own_ref.1) | copy-start | bytes 196612
  12.8 1.9 %collective-permute-start.3 = (f32[4,224,128]{2,1,0:T(8,128)S(1)}, f32[4,224,128]{2,1,0:T(8,128)S(1)}, u32[]{:S(2)}, u32[]{:S(2)}) collective-permute-start(f32[4,224,128]{2,1,0:T(8,128)S(1)} %get-tuple-element.23), channel_id=1, source_target_pairs={{0,2},{2,0},{4,6},{6,4},{8,10},{10,8},{12,14},{14,12},{16,18},{18,... | collective-permute-start | bytes 1376264 | tf_op jit(solution)/shard_map/ppermute | solution.py:284
  12.9 5.4 %copy-start.2 = (bf16[3,3,3,64,128]{4,3,2,1,0:T(8,128)(2,1)S(1)}, bf16[3,3,3,64,128]{4,3,2,1,0:T(8,128)(2,1)}, u32[]{:S(2)}) copy-start(bf16[3,3,3,64,128]{4,3,2,1,0:T(8,128)(2,1)} %param.4) | copy-start | bytes 1327108
  12.9 10.3 %collective-permute-start.7 = (bf16[4,128,256]{2,1,0:T(8,128)(2,1)S(1)}, bf16[4,128,256]{2,1,0:T(8,128)(2,1)S(1)}, u32[]{:S(2)}, u32[]{:S(2)}) collective-permute-start(bf16[4,128,256]{2,1,0:T(8,128)(2,1)S(1)} %slice.67), channel_id=1, source_target_pairs={{0,2},{1,3},{2,4},{3,5},{4,6},{5,7},{6,8},{7,9},{8,10},{9,11},{10,... | collective-permute-start | bytes 786440 | tf_op jit(solution)/shard_map/ppermute | solution.py:280
  14.8 8.3 %collective-permute-start.6 = (f16[224,128]{1,0:T(8,128)(2,1)S(1)}, f16[224,128]{1,0:T(8,128)(2,1)S(1)}, u32[]{:S(2)}, u32[]{:S(2)}) collective-permute-start(f16[224,128]{1,0:T(8,128)(2,1)S(1)} %get-tuple-element.44), channel_id=1, source_target_pairs={{0,4},{1,5},{2,6},{3,7},{4,0},{5,1},{6,2},{7,3},{8,12},{9,13},{10,... | collective-permute-start | bytes 172040 | tf_op jit(solution)/shard_map/ppermute | solution.py:295
  14.9 8.2 %collective-permute-start.5 = (f16[224,128]{1,0:T(8,128)(2,1)S(1)}, f16[224,128]{1,0:T(8,128)(2,1)S(1)}, u32[]{:S(2)}, u32[]{:S(2)}) collective-permute-start(f16[224,128]{1,0:T(8,128)(2,1)S(1)} %get-tuple-element.45), channel_id=1, source_target_pairs={{0,1},{1,0},{2,3},{3,2},{4,5},{5,4},{6,7},{7,6},{8,9},{9,8},{10,11... | collective-permute-start | bytes 172040 | tf_op jit(solution)/shard_map/ppermute | solution.py:295
  16.2 6.9 %collective-permute-start.4 = (f16[224,128]{1,0:T(8,128)(2,1)S(1)}, f16[224,128]{1,0:T(8,128)(2,1)S(1)}, u32[]{:S(2)}, u32[]{:S(2)}) collective-permute-start(f16[224,128]{1,0:T(8,128)(2,1)S(1)} %get-tuple-element.43), channel_id=1, source_target_pairs={{0,5},{1,4},{2,7},{3,6},{4,1},{5,0},{6,3},{7,2},{8,13},{9,12},{10,... | collective-permute-start | bytes 172040 | tf_op jit(solution)/shard_map/ppermute | solution.py:295
  23.3 6.3 %collective-permute-start.10 = (f16[224,128]{1,0:T(8,128)(2,1)S(1)}, f16[224,128]{1,0:T(8,128)(2,1)S(1)}, u32[]{:S(2)}, u32[]{:S(2)}) collective-permute-start(f16[224,128]{1,0:T(8,128)(2,1)S(1)} %get-tuple-element.38), channel_id=1, source_target_pairs={{0,24},{2,26},{4,28},{6,30},{8,16},{10,18},{12,20},{14,22},{16,8},... | collective-permute-start | bytes 172040 | tf_op jit(solution)/shard_map/ppermute | solution.py:284
  25.4 5.5 %collective-permute-start.9 = (f16[224,128]{1,0:T(8,128)(2,1)S(1)}, f16[224,128]{1,0:T(8,128)(2,1)S(1)}, u32[]{:S(2)}, u32[]{:S(2)}) collective-permute-start(f16[224,128]{1,0:T(8,128)(2,1)S(1)} %get-tuple-element.38), channel_id=1, source_target_pairs={{0,16},{2,18},{4,20},{6,22},{8,24},{10,26},{12,28},{14,30},{16,0},... | collective-permute-start | bytes 172040 | tf_op jit(solution)/shard_map/ppermute | solution.py:284
  25.4 5.5 %collective-permute-start.8 = (f16[224,128]{1,0:T(8,128)(2,1)S(1)}, f16[224,128]{1,0:T(8,128)(2,1)S(1)}, u32[]{:S(2)}, u32[]{:S(2)}) collective-permute-start(f16[224,128]{1,0:T(8,128)(2,1)S(1)} %get-tuple-element.38), channel_id=1, source_target_pairs={{0,8},{2,10},{4,12},{6,14},{8,0},{10,2},{12,4},{14,6},{16,24},{18,... | collective-permute-start | bytes 172040 | tf_op jit(solution)/shard_map/ppermute | solution.py:284
  27.9 6.7 %collective-permute-start.14 = (bf16[6,128,128]{2,1,0:T(8,128)(2,1)S(1)}, bf16[6,128,128]{2,1,0:T(8,128)(2,1)S(1)}, u32[]{:S(2)}, u32[]{:S(2)}) collective-permute-start(bf16[6,128,128]{2,1,0:T(8,128)(2,1)S(1)} %pad_maximum_fusion.1), channel_id=1, source_target_pairs={{0,1},{1,0},{2,3},{3,2},{4,5},{5,4},{6,7},{7,6},{8,9},{9,8},{10,11... | collective-permute-start | bytes 589832 | tf_op jit(solution)/shard_map/ppermute | solution.py:280
  31.0 5.4 %collective-permute-start.11 = (f16[224,128]{1,0:T(8,128)(2,1)S(1)}, f16[224,128]{1,0:T(8,128)(2,1)S(1)}, u32[]{:S(2)}, u32[]{:S(2)}) collective-permute-start(f16[224,128]{1,0:T(8,128)(2,1)S(1)} %select_convert_fusion), channel_id=1, source_target_pairs={{0,1},{1,0},{2,3},{3,2},{4,5},{5,4},{6,7},{7,6},{8,9},{9,8},{10,11... | collective-permute-start | bytes 172040 | tf_op jit(solution)/shard_map/ppermute | solution.py:295
  32.6 4.2 %collective-permute-start.12 = (f16[224,128]{1,0:T(8,128)(2,1)S(1)}, f16[224,128]{1,0:T(8,128)(2,1)S(1)}, u32[]{:S(2)}, u32[]{:S(2)}) collective-permute-start(f16[224,128]{1,0:T(8,128)(2,1)S(1)} %select_convert_fusion), channel_id=1, source_target_pairs={{0,4},{1,5},{2,6},{3,7},{4,0},{5,1},{6,2},{7,3},{8,12},{9,13},{10,... | collective-permute-start | bytes 172040 | tf_op jit(solution)/shard_map/ppermute | solution.py:295
  32.7 5.1 %collective-permute-start.13 = (f16[224,128]{1,0:T(8,128)(2,1)S(1)}, f16[224,128]{1,0:T(8,128)(2,1)S(1)}, u32[]{:S(2)}, u32[]{:S(2)}) collective-permute-start(f16[224,128]{1,0:T(8,128)(2,1)S(1)} %select_convert_fusion), channel_id=1, source_target_pairs={{0,5},{1,4},{2,7},{3,6},{4,1},{5,0},{6,3},{7,2},{8,13},{9,12},{10,... | collective-permute-start | bytes 172040 | tf_op jit(solution)/shard_map/ppermute | solution.py:295
  37.9 1.6 %collective-permute-start.15 = (f16[4,224,128]{2,1,0:T(8,128)(2,1)S(1)}, f16[4,224,128]{2,1,0:T(8,128)(2,1)S(1)}, u32[]{:S(2)}, u32[]{:S(2)}) collective-permute-start(f16[4,224,128]{2,1,0:T(8,128)(2,1)S(1)} %pad_maximum_fusion), channel_id=1, source_target_pairs={{0,2},{2,0},{4,6},{6,4},{8,10},{10,8},{12,14},{14,12},{16,18},{18,... | collective-permute-start | bytes 688136 | tf_op jit(solution)/shard_map/ppermute | solution.py:284
where the time goes:
time: 40.5 us; the launch traced here: 40.3 us
  starting transfers between devices  20.9 us (52%)
  waiting for transfers between devices  8.24 us (20%)
  Pallas kernels  7.67 us (19%)
  local copies, waits for them, and re-layouts  1.93 us (5%)
  between operations  0.88 us (2%)
  other arithmetic  0.65 us (2%)
    ppermute x5, starting transfers between devices, shifted(): return lax.ppermute(array, ('sp', 'gz'), pairs)  9.21 us
    ppermute x6, starting transfers between devices, swapped_in_plane(): return lax.ppermute(array, ('sp', 'gz'), pairs)  7.1 us
    pallas_call x4, Pallas kernels, call(): pl.pallas_call(body, out_shape=outs, in_specs=[pl.BlockSpec(memory_space=...  6 us
    ppermute x5, starting transfers between devices, swapped(): lax.ppermute(array, 'sp', [(i, i ^ flip) for i in range(lax.axis_size('sp...  4.59 us
    ppermute x6, waiting for transfers between devices, swapped_in_plane(): return lax.ppermute(array, ('sp', 'gz'), pairs)  3.79 us
    ppermute x5, waiting for transfers between devices, swapped(): lax.ppermute(array, 'sp', [(i, i ^ flip) for i in range(lax.axis_size('sp...  3.45 us
    unnamed x6, local copies, waits for them, and re-layouts  1.89 us
    pallas_call x2, Pallas kernels, per_device(): pl.pallas_call(functools.partial(assemble_body, 1.0 / math.sqrt(out_cells...  1.68 us
  transfers between devices with their start and end apart: 16, of which 9 were waited for; matrix products, arithmetic and copies ran while one was open for 1% of the time, Pallas kernels for 14%

commit v1 on v0

--- a/solution.py
+++ b/solution.py
@@ -315,7 +315,8 @@
 
 
 def sum_over_plane(keep, got, each, parts):
-    level = jnp.maximum(keep[0, each : each + 1], got[0, each : each + 1]) + 1.0
+    got, level = decoded(got, each)
+    level = jnp.maximum(keep[0, each : each + 1], level[0]) + 1.0
     parts_got = {
         k: swapped_in_plane(coded(keep[k] + got[k], level, each), k) for k in partners(parts)
     }
@@ -330,7 +331,7 @@
 def sum_over_lines(total, level, each):
     quads = lax.axis_size("sp") // 4
     message = coded(total, level, each)
-    others = {k: swapped(message, 4 * k) for k in range(quads - 1, 0, -1)}
+    others = {k: swapped(message, 4 * k) for k in range(1, quads)}
     terms = [decoded(message, each)] + [decoded(others[k], each) for k in range(1, quads)]
     while len(terms) > 1:
         terms = [
@@ -396,9 +397,8 @@
         [pltpu.VMEM((8, channels, cells), BF), pltpu.VMEM((rows, out_channels), F32)],
         500000000,
     )
-    plane, send = in_order(classes[4:], send)
-    from_z = shifted(plane, 1, 0)
-    got = swapped(send, 1)
+    from_z = shifted(classes[4:], 1, 0)
+    got = swapped(coded(send, send[0, each : each + 1], each), 1)
     weights = weight.reshape(27, width, out_channels)
     spread = pltpu.VMEM((27 * channels, out_channels), BF)
     volume_grad = call(

time: 40.5 us -> 40.5 us (level)
    ppermute x5, waiting for transfers between devices: 3.45 us -> 4.96 us  [swapped(): lax.ppermute(array, 'sp', [(i, i ^ flip) for i in range(lax.axis_size('sp...]
    ppermute x6, waiting for transfers between devices: 3.79 us -> 2.31 us  [swapped_in_plane(): return lax.ppermute(array, ('sp', 'gz'), pairs)]
  transfers between devices with their start and end apart: 16 -> 16, of which waited for: 9 -> 7; matrix products, arithmetic and copies ran while one was open for 1% -> 2% of each run, Pallas kernels for 14% -> 17%
where the time goes in v1:
time: 40.5 us; the launch traced here: 40.3 us
  starting transfers between devices  20.9 us (52%)
  waiting for transfers between devices  7.94 us (20%)
  Pallas kernels  7.68 us (19%)
  local copies, waits for them, and re-layouts  1.93 us (5%)
  between operations  0.91 us (2%)
  other arithmetic  0.86 us (2%)
    ppermute x5, starting transfers between devices, shifted(): return lax.ppermute(array, ('sp', 'gz'), pairs)  9.1 us
    ppermute x6, starting transfers between devices, swapped_in_plane(): return lax.ppermute(array, ('sp', 'gz'), pairs)  7.1 us
    pallas_call x4, Pallas kernels, call(): pl.pallas_call(body, out_shape=outs, in_specs=[pl.BlockSpec(memory_space=...  6 us
    ppermute x5, waiting for transfers between devices, swapped(): lax.ppermute(array, 'sp', [(i, i ^ flip) for i in range(lax.axis_size('sp...  4.96 us
    ppermute x5, starting transfers between devices, swapped(): lax.ppermute(array, 'sp', [(i, i ^ flip) for i in range(lax.axis_size('sp...  4.74 us
    ppermute x6, waiting for transfers between devices, swapped_in_plane(): return lax.ppermute(array, ('sp', 'gz'), pairs)  2.31 us
    unnamed x6, local copies, waits for them, and re-layouts  1.89 us
    pallas_call x2, Pallas kernels, per_device(): pl.pallas_call(functools.partial(assemble_body, 1.0 / math.sqrt(out_cells...  1.68 us
  transfers between devices with their start and end apart: 16, of which 7 were waited for; matrix products, arithmetic and copies ran while one was open for 2% of the time, Pallas kernels for 17%

profile of v1, /device:TPU:0, one launch (start us, length us, event | category | flops | bytes accessed | tf_op | source)
XLA Modules:
  0.0 40.3 jit_solution(7741943903061594396)
XLA Ops:
  0.6 5.5 %collective-permute-start = (bf16[128,1,2,128]{3,2,1,0:T(2,128)(2,1)}, bf16[128,1,2,128]{3,2,1,0:T(2,128)(2,1)S(1)}, u32[]{:S(2)}, u32[]{:S(2)}) collective-permute-start(bf16[128,1,2,128]{3,2,1,0:T(2,128)(2,1)} %own_ref.1), channel_id=1, source_target_pairs={{0,30},{1,31},{2,0},{3,1},{4,2},{5,3},{6,4},{7,5},{8,6},{9,7},{10,... | collective-permute-start | bytes 196616 | tf_op jit(solution)/shard_map/ppermute | solution.py:280
  6.1 1.5 %collective-permute-start.1 = (bf16[128,1,2,128]{3,2,1,0:T(2,128)(2,1)}, bf16[128,1,2,128]{3,2,1,0:T(2,128)(2,1)S(1)}, u32[]{:S(2)}, u32[]{:S(2)}) collective-permute-start(bf16[128,1,2,128]{3,2,1,0:T(2,128)(2,1)} %own_ref.1), channel_id=1, source_target_pairs={{0,1},{1,0},{2,3},{3,2},{4,5},{5,4},{6,7},{7,6},{8,9},{9,8},{10,11... | collective-permute-start | bytes 196616 | tf_op jit(solution)/shard_map/ppermute | solution.py:280
  8.0 1.0 %copy-done = bf16[128,2,4,256]{3,2,1,0:T(4,128)(2,1)S(1)} copy-done((bf16[128,2,4,256]{3,2,1,0:T(4,128)(2,1)S(1)}, bf16[128,2,4,256]{3,2,1,0:T(4,128)(2,1)}, u32[]{:S(2)}) %copy-start) | copy-done | bytes 524312
  9.0 0.8 %copy-done.1 = bf16[128,1,2,128]{3,2,1,0:T(2,128)(2,1)S(1)} copy-done((bf16[128,1,2,128]{3,2,1,0:T(2,128)(2,1)S(1)}, bf16[128,1,2,128]{3,2,1,0:T(2,128)(2,1)}, u32[]{:S(2)}) %copy-start.1) | copy-done | bytes 65560
  9.9 0.6 %shard_map.58 = (bf16[8,128,256]{2,1,0:T(8,128)(2,1)S(1)}, bf16[2,128,256]{2,1,0:T(8,128)(2,1)S(1)}) custom-call(bf16[128,2,4,256]{3,2,1,0:T(4,128)(2,1)S(1)} %copy-done, bf16[128,1,2,128]{3,2,1,0:T(2,128)(2,1)S(1)} %copy-done.1), custom_call_target="tpu_custom_call" | custom-call | bytes 4000000 | tf_op jit(solution)/shard_map/pallas_call | solution.py:353
  10.9 0.7 %collective-permute-done.2.up_c_ref = bf16[128,1,2,128]{3,2,1,0:T(2,128)(2,1)S(1)} collective-permute-done((bf16[128,1,2,128]{3,2,1,0:T(2,128)(2,1)}, bf16[128,1,2,128]{3,2,1,0:T(2,128)(2,1)S(1)}, u32[]{:S(2)}, u32[]{:S(2)}) %collective-permute-start.2) | collective-permute-done | bytes 65568 | tf_op jit(solution)/shard_map/ppermute | solution.py:280
  11.5 1.3 %shard_map.59 = (bf16[6,128,256]{2,1,0:T(8,128)(2,1)S(1)}, f32[4,224,128]{2,1,0:T(8,128)S(1)}, f32[4,224,128]{2,1,0:T(8,128)S(1)}) custom-call(bf16[8,128,256]{2,1,0:T(8,128)(2,1)S(1)} %get-tuple-element.17.class_ref, bf16[2,128,256]{2,1,0:T(8,128)(2,1)S(1)} %get-tuple-element.18.own_ref, bf16[128,1,2,128]{3,2,1,0:T(2,128)(2,1)S(1)} %collective-permute-done.up_z_ref, ...), custom_call_target="tpu_custom_call" | custom-call | flops 500000000 | bytes 4000000 | tf_op jit(solution)/shard_map/pallas_call | solution.py:353
  13.0 1.4 %collective-permute-done.3 = f16[4,224,128]{2,1,0:T(8,128)(2,1)S(1)} collective-permute-done((f16[4,224,128]{2,1,0:T(8,128)(2,1)S(1)}, f16[4,224,128]{2,1,0:T(8,128)(2,1)S(1)}, u32[]{:S(2)}, u32[]{:S(2)}) %collective-permute-start.3) | collective-permute-done | bytes 229408 | tf_op jit(solution)/shard_map/ppermute | solution.py:284
  14.8 1.3 %collective-permute-start.5 = (f16[224,128]{1,0:T(8,128)(2,1)S(1)}, f16[224,128]{1,0:T(8,128)(2,1)S(1)}, u32[]{:S(2)}, u32[]{:S(2)}) collective-permute-start(f16[224,128]{1,0:T(8,128)(2,1)S(1)} %get-tuple-element.41), channel_id=1, source_target_pairs={{0,1},{1,0},{2,3},{3,2},{4,5},{5,4},{6,7},{7,6},{8,9},{9,8},{10,11... | collective-permute-start | bytes 172040 | tf_op jit(solution)/shard_map/ppermute | solution.py:295
  16.1 2.2 %collective-permute-start.4 = (f16[224,128]{1,0:T(8,128)(2,1)S(1)}, f16[224,128]{1,0:T(8,128)(2,1)S(1)}, u32[]{:S(2)}, u32[]{:S(2)}) collective-permute-start(f16[224,128]{1,0:T(8,128)(2,1)S(1)} %get-tuple-element.39), channel_id=1, source_target_pairs={{0,5},{1,4},{2,7},{3,6},{4,1},{5,0},{6,3},{7,2},{8,13},{9,12},{10,... | collective-permute-start | bytes 172040 | tf_op jit(solution)/shard_map/ppermute | solution.py:295
  18.3 2.3 %shard_map.60 = bf16[128,2,4,256]{3,2,1,0:T(4,128)(2,1)} custom-call(bf16[6,128,256]{2,1,0:T(8,128)(2,1)S(1)} %get-tuple-element.21.cots_ref, bf16[27,64,128]{2,1,0:T(8,128)(2,1)S(1)} %bitcast.94), custom_call_target="tpu_custom_call" | custom-call | flops 1000000000 | bytes 4000000 | tf_op jit(solution)/shard_map/pallas_call | solution.py:353
  20.6 1.0 %collective-permute-done.6 = f16[224,128]{1,0:T(8,128)(2,1)S(1)} collective-permute-done((f16[224,128]{1,0:T(8,128)(2,1)S(1)}, f16[224,128]{1,0:T(8,128)(2,1)S(1)}, u32[]{:S(2)}, u32[]{:S(2)}) %collective-permute-start.6) | collective-permute-done | bytes 57376 | tf_op jit(solution)/shard_map/ppermute | solution.py:295
  21.8 4.0 %collective-permute-start.10 = (f16[224,128]{1,0:T(8,128)(2,1)S(1)}, f16[224,128]{1,0:T(8,128)(2,1)S(1)}, u32[]{:S(2)}, u32[]{:S(2)}) collective-permute-start(f16[224,128]{1,0:T(8,128)(2,1)S(1)} %get-tuple-element.34), channel_id=1, source_target_pairs={{0,24},{2,26},{4,28},{6,30},{8,16},{10,18},{12,20},{14,22},{16,8},... | collective-permute-start | bytes 172040 | tf_op jit(solution)/shard_map/ppermute | solution.py:284
  25.8 0.6 %collective-permute-start.8 = (f16[224,128]{1,0:T(8,128)(2,1)S(1)}, f16[224,128]{1,0:T(8,128)(2,1)S(1)}, u32[]{:S(2)}, u32[]{:S(2)}) collective-permute-start(f16[224,128]{1,0:T(8,128)(2,1)S(1)} %get-tuple-element.34), channel_id=1, source_target_pairs={{0,8},{2,10},{4,12},{6,14},{8,0},{10,2},{12,4},{14,6},{16,24},{18,... | collective-permute-start | bytes 172040 | tf_op jit(solution)/shard_map/ppermute | solution.py:284
  26.4 1.4 %collective-permute-start.14 = (bf16[6,128,128]{2,1,0:T(8,128)(2,1)S(1)}, bf16[6,128,128]{2,1,0:T(8,128)(2,1)S(1)}, u32[]{:S(2)}, u32[]{:S(2)}) collective-permute-start(bf16[6,128,128]{2,1,0:T(8,128)(2,1)S(1)} %pad_maximum_fusion.1), channel_id=1, source_target_pairs={{0,1},{1,0},{2,3},{3,2},{4,5},{5,4},{6,7},{7,6},{8,9},{9,8},{10,11... | collective-permute-start | bytes 589832 | tf_op jit(solution)/shard_map/ppermute | solution.py:280
  28.2 2.6 %collective-permute-done.9 = f16[224,128]{1,0:T(8,128)(2,1)S(1)} collective-permute-done((f16[224,128]{1,0:T(8,128)(2,1)S(1)}, f16[224,128]{1,0:T(8,128)(2,1)S(1)}, u32[]{:S(2)}, u32[]{:S(2)}) %collective-permute-start.9) | collective-permute-done | bytes 57376 | tf_op jit(solution)/shard_map/ppermute | solution.py:284
  31.0 1.3 %collective-permute-start.11 = (f16[224,128]{1,0:T(8,128)(2,1)S(1)}, f16[224,128]{1,0:T(8,128)(2,1)S(1)}, u32[]{:S(2)}, u32[]{:S(2)}) collective-permute-start(f16[224,128]{1,0:T(8,128)(2,1)S(1)} %select_convert_fusion.1), channel_id=1, source_target_pairs={{0,1},{1,0},{2,3},{3,2},{4,5},{5,4},{6,7},{7,6},{8,9},{9,8},{10,11... | collective-permute-start | bytes 172040 | tf_op jit(solution)/shard_map/ppermute | solution.py:295
  32.3 0.4 collective-permute-start.12
  32.7 1.9 %collective-permute-start.13 = (f16[224,128]{1,0:T(8,128)(2,1)S(1)}, f16[224,128]{1,0:T(8,128)(2,1)S(1)}, u32[]{:S(2)}, u32[]{:S(2)}) collective-permute-start(f16[224,128]{1,0:T(8,128)(2,1)S(1)} %select_convert_fusion.1), channel_id=1, source_target_pairs={{0,5},{1,4},{2,7},{3,6},{4,1},{5,0},{6,3},{7,2},{8,13},{9,12},{10,... | collective-permute-start | bytes 172040 | tf_op jit(solution)/shard_map/ppermute | solution.py:295
  34.6 1.9 %shard_map.61 = bf16[128,1,2,128]{3,2,1,0:T(2,128)(2,1)} custom-call(bf16[8,128,256]{2,1,0:T(8,128)(2,1)S(1)} %get-tuple-element.17.class_ref, bf16[4,128,256]{2,1,0:T(8,128)(2,1)S(1)} %collective-permute-done.7.from_z_ref, bf16[6,128,128]{2,1,0:T(8,128)(2,1)S(1)} %collective-permute-done.14.from_y_ref, bf16[27,64,128]{2,1,0:T(8,128)(2,1)S(1)} %bitcast.95), custom_call_target="tpu_custom_call" | custom-call | flops 1000000000 | bytes 4000000 | tf_op jit(solution)/shard_map/pallas_call | solution.py:353
  36.5 1.3 %collective-permute-done.13 = f16[224,128]{1,0:T(8,128)(2,1)S(1)} collective-permute-done((f16[224,128]{1,0:T(8,128)(2,1)S(1)}, f16[224,128]{1,0:T(8,128)(2,1)S(1)}, u32[]{:S(2)}, u32[]{:S(2)}) %collective-permute-start.13) | collective-permute-done | bytes 57376 | tf_op jit(solution)/shard_map/ppermute | solution.py:295
  38.0 0.8 %shard_map.62.refs_4_ = f32[1728,128]{1,0:T(8,128)} custom-call(f32[224,128]{1,0:T(8,128)S(1)} %convert_element_type.96.refs_0_, f32[224,128]{1,0:T(8,128)S(1)} %convert_element_type.97.refs_1_, f32[224,128]{1,0:T(8,128)S(1)} %convert_element_type.98.refs_2_, f32[224,128]{1,0:T(8,128)S(1)} %convert_element_type.99.refs_3_), custom_call_target="tpu_custom_call" | custom-call | flops 1000000 | bytes 1000000 | tf_op jit(solution)/shard_map/pallas_call | solution.py:434
  38.8 0.6 %collective-permute-done.15 = f16[4,224,128]{2,1,0:T(8,128)(2,1)S(1)} collective-permute-done((f16[4,224,128]{2,1,0:T(8,128)(2,1)S(1)}, f16[4,224,128]{2,1,0:T(8,128)(2,1)S(1)}, u32[]{:S(2)}, u32[]{:S(2)}) %collective-permute-start.15) | collective-permute-done | bytes 229408 | tf_op jit(solution)/shard_map/ppermute | solution.py:284
  39.4 0.8 %shard_map.63 = f32[1728,128]{1,0:T(8,128)} custom-call(f32[224,128]{1,0:T(8,128)S(1)} %get-tuple-element.49.refs_0_, f32[224,128]{1,0:T(8,128)S(1)} %get-tuple-element.48.refs_1_, f32[224,128]{1,0:T(8,128)S(1)} %get-tuple-element.47.refs_2_, f32[224,128]{1,0:T(8,128)S(1)} %get-tuple-element.46.refs_3_, ...), custom_call_target="tpu_custom_call", output_to_operand_aliasing={{}: (4, {})} | custom-call | flops 1000000 | bytes 1000000 | tf_op jit(solution)/shard_map/pallas_call | solution.py:434
  (49 shorter events, 2.2 us)
Async XLA Ops:
  0.6 10.2 %collective-permute-start = (bf16[128,1,2,128]{3,2,1,0:T(2,128)(2,1)}, bf16[128,1,2,128]{3,2,1,0:T(2,128)(2,1)S(1)}, u32[]{:S(2)}, u32[]{:S(2)}) collective-permute-start(bf16[128,1,2,128]{3,2,1,0:T(2,128)(2,1)} %own_ref.1), channel_id=1, source_target_pairs={{0,30},{1,31},{2,0},{3,1},{4,2},{5,3},{6,4},{7,5},{8,6},{9,7},{10,... | collective-permute-start | bytes 196616 | tf_op jit(solution)/shard_map/ppermute | solution.py:280
  6.1 4.7 %collective-permute-start.1 = (bf16[128,1,2,128]{3,2,1,0:T(2,128)(2,1)}, bf16[128,1,2,128]{3,2,1,0:T(2,128)(2,1)S(1)}, u32[]{:S(2)}, u32[]{:S(2)}) collective-permute-start(bf16[128,1,2,128]{3,2,1,0:T(2,128)(2,1)} %own_ref.1), channel_id=1, source_target_pairs={{0,1},{1,0},{2,3},{3,2},{4,5},{5,4},{6,7},{7,6},{8,9},{9,8},{10,11... | collective-permute-start | bytes 196616 | tf_op jit(solution)/shard_map/ppermute | solution.py:280
  7.6 3.9 %collective-permute-start.2 = (bf16[128,1,2,128]{3,2,1,0:T(2,128)(2,1)}, bf16[128,1,2,128]{3,2,1,0:T(2,128)(2,1)S(1)}, u32[]{:S(2)}, u32[]{:S(2)}) collective-permute-start(bf16[128,1,2,128]{3,2,1,0:T(2,128)(2,1)} %own_ref.1), channel_id=1, source_target_pairs={{0,31},{1,30},{2,1},{3,0},{4,3},{5,2},{6,5},{7,4},{8,7},{9,6},{10,... | collective-permute-start | bytes 196616 | tf_op jit(solution)/shard_map/ppermute | solution.py:280
  8.0 1.0 %copy-start = (bf16[128,2,4,256]{3,2,1,0:T(4,128)(2,1)S(1)}, bf16[128,2,4,256]{3,2,1,0:T(4,128)(2,1)}, u32[]{:S(2)}) copy-start(bf16[128,2,4,256]{3,2,1,0:T(4,128)(2,1)} %vol_ref.1) | copy-start | bytes 1572868
  9.0 0.8 %copy-start.1 = (bf16[128,1,2,128]{3,2,1,0:T(2,128)(2,1)S(1)}, bf16[128,1,2,128]{3,2,1,0:T(2,128)(2,1)}, u32[]{:S(2)}) copy-start(bf16[128,1,2,128]{3,2,1,0:T(2,128)(2,1)} %own_ref.1) | copy-start | bytes 196612
  10.5 11.2 %collective-permute-start.7 = (bf16[4,128,256]{2,1,0:T(8,128)(2,1)S(1)}, bf16[4,128,256]{2,1,0:T(8,128)(2,1)S(1)}, u32[]{:S(2)}, u32[]{:S(2)}) collective-permute-start(bf16[4,128,256]{2,1,0:T(8,128)(2,1)S(1)} %slice.88), channel_id=1, source_target_pairs={{0,2},{1,3},{2,4},{3,5},{4,6},{5,7},{6,8},{7,9},{8,10},{9,11},{10,... | collective-permute-start | bytes 786440 | tf_op jit(solution)/shard_map/ppermute | solution.py:280
  12.9 1.6 %collective-permute-start.3 = (f16[4,224,128]{2,1,0:T(8,128)(2,1)S(1)}, f16[4,224,128]{2,1,0:T(8,128)(2,1)S(1)}, u32[]{:S(2)}, u32[]{:S(2)}) collective-permute-start(f16[4,224,128]{2,1,0:T(8,128)(2,1)S(1)} %select_convert_fusion), channel_id=1, source_target_pairs={{0,2},{2,0},{4,6},{6,4},{8,10},{10,8},{12,14},{14,12},{16,18},{18,... | collective-permute-start | bytes 688136 | tf_op jit(solution)/shard_map/ppermute | solution.py:284
  14.6 3.7 %copy-start.2 = (bf16[3,3,3,64,128]{4,3,2,1,0:T(8,128)(2,1)S(1)}, bf16[3,3,3,64,128]{4,3,2,1,0:T(8,128)(2,1)}, u32[]{:S(2)}) copy-start(bf16[3,3,3,64,128]{4,3,2,1,0:T(8,128)(2,1)} %param.4) | copy-start | bytes 1327108
  14.7 6.8 %collective-permute-start.6 = (f16[224,128]{1,0:T(8,128)(2,1)S(1)}, f16[224,128]{1,0:T(8,128)(2,1)S(1)}, u32[]{:S(2)}, u32[]{:S(2)}) collective-permute-start(f16[224,128]{1,0:T(8,128)(2,1)S(1)} %get-tuple-element.40), channel_id=1, source_target_pairs={{0,4},{1,5},{2,6},{3,7},{4,0},{5,1},{6,2},{7,3},{8,12},{9,13},{10,... | collective-permute-start | bytes 172040 | tf_op jit(solution)/shard_map/ppermute | solution.py:295
  14.8 6.7 %collective-permute-start.5 = (f16[224,128]{1,0:T(8,128)(2,1)S(1)}, f16[224,128]{1,0:T(8,128)(2,1)S(1)}, u32[]{:S(2)}, u32[]{:S(2)}) collective-permute-start(f16[224,128]{1,0:T(8,128)(2,1)S(1)} %get-tuple-element.41), channel_id=1, source_target_pairs={{0,1},{1,0},{2,3},{3,2},{4,5},{5,4},{6,7},{7,6},{8,9},{9,8},{10,11... | collective-permute-start | bytes 172040 | tf_op jit(solution)/shard_map/ppermute | solution.py:295
  16.1 5.5 %collective-permute-start.4 = (f16[224,128]{1,0:T(8,128)(2,1)S(1)}, f16[224,128]{1,0:T(8,128)(2,1)S(1)}, u32[]{:S(2)}, u32[]{:S(2)}) collective-permute-start(f16[224,128]{1,0:T(8,128)(2,1)S(1)} %get-tuple-element.39), channel_id=1, source_target_pairs={{0,5},{1,4},{2,7},{3,6},{4,1},{5,0},{6,3},{7,2},{8,13},{9,12},{10,... | collective-permute-start | bytes 172040 | tf_op jit(solution)/shard_map/ppermute | solution.py:295
  21.8 6.4 %collective-permute-start.10 = (f16[224,128]{1,0:T(8,128)(2,1)S(1)}, f16[224,128]{1,0:T(8,128)(2,1)S(1)}, u32[]{:S(2)}, u32[]{:S(2)}) collective-permute-start(f16[224,128]{1,0:T(8,128)(2,1)S(1)} %get-tuple-element.34), channel_id=1, source_target_pairs={{0,24},{2,26},{4,28},{6,30},{8,16},{10,18},{12,20},{14,22},{16,8},... | collective-permute-start | bytes 172040 | tf_op jit(solution)/shard_map/ppermute | solution.py:284
  25.7 5.1 %collective-permute-start.9 = (f16[224,128]{1,0:T(8,128)(2,1)S(1)}, f16[224,128]{1,0:T(8,128)(2,1)S(1)}, u32[]{:S(2)}, u32[]{:S(2)}) collective-permute-start(f16[224,128]{1,0:T(8,128)(2,1)S(1)} %get-tuple-element.34), channel_id=1, source_target_pairs={{0,16},{2,18},{4,20},{6,22},{8,24},{10,26},{12,28},{14,30},{16,0},... | collective-permute-start | bytes 172040 | tf_op jit(solution)/shard_map/ppermute | solution.py:284
  25.8 5.1 %collective-permute-start.8 = (f16[224,128]{1,0:T(8,128)(2,1)S(1)}, f16[224,128]{1,0:T(8,128)(2,1)S(1)}, u32[]{:S(2)}, u32[]{:S(2)}) collective-permute-start(f16[224,128]{1,0:T(8,128)(2,1)S(1)} %get-tuple-element.34), channel_id=1, source_target_pairs={{0,8},{2,10},{4,12},{6,14},{8,0},{10,2},{12,4},{14,6},{16,24},{18,... | collective-permute-start | bytes 172040 | tf_op jit(solution)/shard_map/ppermute | solution.py:284
  26.4 8.1 %collective-permute-start.14 = (bf16[6,128,128]{2,1,0:T(8,128)(2,1)S(1)}, bf16[6,128,128]{2,1,0:T(8,128)(2,1)S(1)}, u32[]{:S(2)}, u32[]{:S(2)}) collective-permute-start(bf16[6,128,128]{2,1,0:T(8,128)(2,1)S(1)} %pad_maximum_fusion.1), channel_id=1, source_target_pairs={{0,1},{1,0},{2,3},{3,2},{4,5},{5,4},{6,7},{7,6},{8,9},{9,8},{10,11... | collective-permute-start | bytes 589832 | tf_op jit(solution)/shard_map/ppermute | solution.py:280
  31.0 5.4 %collective-permute-start.11 = (f16[224,128]{1,0:T(8,128)(2,1)S(1)}, f16[224,128]{1,0:T(8,128)(2,1)S(1)}, u32[]{:S(2)}, u32[]{:S(2)}) collective-permute-start(f16[224,128]{1,0:T(8,128)(2,1)S(1)} %select_convert_fusion.1), channel_id=1, source_target_pairs={{0,1},{1,0},{2,3},{3,2},{4,5},{5,4},{6,7},{7,6},{8,9},{9,8},{10,11... | collective-permute-start | bytes 172040 | tf_op jit(solution)/shard_map/ppermute | solution.py:295
  32.3 4.2 %collective-permute-start.12 = (f16[224,128]{1,0:T(8,128)(2,1)S(1)}, f16[224,128]{1,0:T(8,128)(2,1)S(1)}, u32[]{:S(2)}, u32[]{:S(2)}) collective-permute-start(f16[224,128]{1,0:T(8,128)(2,1)S(1)} %select_convert_fusion.1), channel_id=1, source_target_pairs={{0,4},{1,5},{2,6},{3,7},{4,0},{5,1},{6,2},{7,3},{8,12},{9,13},{10,... | collective-permute-start | bytes 172040 | tf_op jit(solution)/shard_map/ppermute | solution.py:295
  32.7 5.1 %collective-permute-start.13 = (f16[224,128]{1,0:T(8,128)(2,1)S(1)}, f16[224,128]{1,0:T(8,128)(2,1)S(1)}, u32[]{:S(2)}, u32[]{:S(2)}) collective-permute-start(f16[224,128]{1,0:T(8,128)(2,1)S(1)} %select_convert_fusion.1), channel_id=1, source_target_pairs={{0,5},{1,4},{2,7},{3,6},{4,1},{5,0},{6,3},{7,2},{8,13},{9,12},{10,... | collective-permute-start | bytes 172040 | tf_op jit(solution)/shard_map/ppermute | solution.py:295
  37.8 1.6 %collective-permute-start.15 = (f16[4,224,128]{2,1,0:T(8,128)(2,1)S(1)}, f16[4,224,128]{2,1,0:T(8,128)(2,1)S(1)}, u32[]{:S(2)}, u32[]{:S(2)}) collective-permute-start(f16[4,224,128]{2,1,0:T(8,128)(2,1)S(1)} %pad_maximum_fusion), channel_id=1, source_target_pairs={{0,2},{2,0},{4,6},{6,4},{8,10},{10,8},{12,14},{14,12},{16,18},{18,... | collective-permute-start | bytes 688136 | tf_op jit(solution)/shard_map/ppermute | solution.py:284
